TPU v7x, 256 devices: a whole 4x4x8 slice. The times are simulated.
256 devices in a mesh: val: 8 (over z_lo, core), cond: 32 (over z_hi, x, y).
Axes of the slice: x: 4, y: 4, z: 8 (z_hi: 2, z_lo: 4; z = z_hi * 4 + z_lo), core: 2. Of those that a mesh axis runs over, the one named last changes fastest.
Arguments:
- conduction: bfloat16 [2, 512, 96, 9216], P(None, 'cond', 'val'), may hold values from -3 to 3
- valence: bfloat16 [2, 2, 96, 9216], P(None, None, 'val', 'cond'), may hold values from -3 to 3
- resident: bfloat16 [256, 2, 512, 2048], P('val', None, 'cond'), may hold values from -6 to 6
- interaction: float32 [2048], replicated, may hold values from 0.2 to 2
Outputs:
- kernel_row: bfloat16 [256, 2, 512, 2, 512], P('val', None, 'cond')
All inputs are finite; a program needn't handle non-finite values.
Results may differ from a plain program's by a relative error of at most 0.005.
Values may be sent and summed in bfloat16 or wider, within the bound.
A program may use at most 128 MiB of HBM per device.

v0:
```python
import math

import jax
import jax.numpy as jnp
from jax import lax
from jax.sharding import PartitionSpec as P

GRID = 96
KXY = 16
KZ = 8


def dft_weights(positions, frequencies):
    turns = jnp.mod(positions[:, None] * frequencies[None, :], GRID).astype(jnp.float32)
    angle = turns * (2.0 * math.pi / GRID)
    cosine = jnp.cos(angle)
    sine = jnp.sin(angle)
    return jnp.stack([jnp.stack([cosine, -sine], 1), jnp.stack([sine, cosine], 1)], 0)


def per_device(conduction, valence, resident, interaction):
    cond_block = conduction.shape[1]
    planes_here = conduction.shape[2]
    new_bands = valence.shape[1]
    res_bands = resident.shape[0]
    kept = resident.shape[3]
    highest = lax.Precision.HIGHEST
    first_plane = lax.axis_index("val") * planes_here
    planes = lax.all_gather(valence, "cond", axis=3, tiled=True)
    val_real = planes[0].astype(jnp.float32).reshape(new_bands, planes_here, GRID, GRID)[:, None]
    val_imag = planes[1].astype(jnp.float32).reshape(new_bands, planes_here, GRID, GRID)[:, None]
    cond_real = conduction[0].astype(jnp.float32).reshape(cond_block, planes_here, GRID, GRID)[None]
    cond_imag = conduction[1].astype(jnp.float32).reshape(cond_block, planes_here, GRID, GRID)[None]
    dens_real = val_real * cond_real + val_imag * cond_imag
    dens_imag = val_real * cond_imag - val_imag * cond_real
    grid_points = lax.iota(jnp.int32, GRID)
    z_weights = dft_weights(grid_points, lax.iota(jnp.int32, KZ) - KZ // 2)
    y_weights = dft_weights(grid_points, lax.iota(jnp.int32, KXY) - KXY // 2)
    x_weights = dft_weights(
        first_plane + lax.iota(jnp.int32, planes_here), lax.iota(jnp.int32, KXY) - KXY // 2
    )
    z_spectra = jnp.einsum("vcxyz,zqk->qvcxyk", dens_real, z_weights[0], precision=highest)
    z_spectra = z_spectra + jnp.einsum(
        "vcxyz,zqk->qvcxyk", dens_imag, z_weights[1], precision=highest
    )
    y_spectra = jnp.einsum("pvcxyk,pyqj->qvcxjk", z_spectra, y_weights, precision=highest)
    pairs = new_bands * cond_block
    flattened = y_spectra.reshape(2, pairs, planes_here, KXY * KZ)
    norm = 1.0 / math.sqrt(GRID**3)
    factor = 2.0 / math.sqrt(kept)
    n_cond = lax.axis_size("cond")
    n_val = lax.axis_size("val")
    own_rows = pairs // n_val
    spectra = jnp.einsum("pnxm,pxqi->nqim", flattened, x_weights, precision=highest) * norm
    own_pairs = lax.psum_scatter(
        spectra.reshape(own_rows * lax.axis_size("val"), 2, kept),
        "val",
        scatter_dimension=0,
        tiled=True,
    )
    scaled = (own_pairs * interaction).astype(jnp.bfloat16)
    block_rows = lax.all_gather(scaled, ("val", "cond"), axis=0, tiled=True)
    turned = jnp.stack([block_rows, jnp.stack([-block_rows[:, 1], block_rows[:, 0]], 1)], 0)
    kernel = jnp.einsum("vpcg,qnpg->vqcn", resident, turned, preferred_element_type=jnp.float32)
    kernel = kernel * factor
    kernel = kernel.astype(jnp.bfloat16).reshape(res_bands, 2, cond_block, n_val, n_cond, own_rows)
    kernel = jnp.transpose(kernel, (0, 1, 2, 4, 3, 5))
    kernel = kernel.reshape(res_bands, 2, cond_block, n_cond, new_bands, cond_block)
    kernel = jnp.transpose(kernel, (0, 1, 2, 4, 3, 5))
    return kernel.reshape(res_bands, 2, cond_block, new_bands, n_cond * cond_block)


def solution(mesh):
    in_specs = (
        P(None, "cond", "val", None),
        P(None, None, "val", "cond"),
        P("val", None, "cond", None),
        P(),
    )
    out_specs = P("val", None, "cond", None, None)
    return jax.shard_map(
        per_device, mesh=mesh, in_specs=in_specs, out_specs=out_specs, check_vma=False
    )
```

profile of v0, /device:TPU:1, one launch (start us, length us, event | category | flops | bytes accessed | tf_op | source)
XLA Modules:
  0.0 1334.1 jit_solution(13771608911664314491)
XLA Ops:
  6.5 0.0 all-reduce.3.cloned.1.call-start
  6.5 1.0 copy.27
  7.5 271.3 %all_gather.6 = bf16[2,2,12,9216]{2,1,0,3:T(2,128)(2,1)S(1)} all-gather(bf16[2,2,12,288]{2,1,0,3:T(2,128)(2,1)S(1)} %copy.27), channel_id=1, replica_groups=mesh['val'=8,'cond'=32] {'cond'}, dimensions={3}, use_global_device_ids=true | all-gather | bytes 912384 | tf_op jit(solution)/shard_map/all_gather | solution.py:29
  278.8 7.7 fusion.76
  286.5 8.3 copy.30
  294.7 9.3 copy.28
  304.1 0.1 fusion.70
  304.2 9.8 slice_convert_fusion.1
  314.0 9.4 reshape.412
  323.3 9.3 reshape.410
  332.6 0.1 fusion.68
  332.7 0.0 copy-start
  332.8 0.0 copy-start.1
  332.8 40.6 %fusion = f32[2,8,2,16,12,96]{5,1,4,3,2,0:T(8,128)} fusion(f32[2,12,96,96]{3,2,1,0:T(8,128)S(1)} %copy.30, f32[2,12,96,96]{3,2,1,0:T(8,128)} %copy.28, f32[96,1,8]{0,2,1:T(8,128)S(1)} %get-tuple-element.25, f32[96,1,8]{0,2,1:T(8,128)S(1)} %get-tuple-element.24, f32[16,12,96,96]{3,2,0,1:T(8,128)} %reshape.412, f32[16,12,96,96]{3,2,0,1:T(8,128)} %reshape.410), kind=kOutput, calls=%fused_computation | convolution fusion | flops 690095616 | bytes 18290688 | tf_op jit(solution)/shard_map/vcxyz,zqk->qvcxyk/dot_general | solution.py:43
  373.4 0.0 copy-done
  373.4 0.0 copy-done.1
  373.4 38.3 %add_bitcast_fusion = f32[2,2,16,12,96,8]{4,5,3,2,1,0:T(8,128)S(1)} fusion(f32[2,8,2,16,12,96]{5,1,4,3,2,0:T(8,128)} %fusion, f32[2,12,96,96]{3,2,1,0:T(8,128)S(1)} %copy.30, f32[2,12,96,96]{3,2,1,0:T(8,128)} %copy.28, f32[96,1,8]{0,2,1:T(8,128)S(1)} %get-tuple-element.23, f32[96,1,8]{0,2,1:T(8,128)S(1)} %get-tuple-element.25, ...), kind=kOutput, calls=%fused_computation.33 | convolution fusion | flops 690685440 | bytes 20649984 | tf_op jit(solution)/shard_map/vcxyz,zqk->qvcxyk/dot_general | solution.py:42
  411.7 12.7 fusion.28
  424.4 0.0 copy-start.3
  424.4 0.0 copy-start.2
  424.4 2.5 copy.33
  426.9 2.9 reshape.404
  429.8 2.1 copy.34
  431.9 0.1 fusion.69
  432.1 0.6 fusion.36
  432.7 0.9 reshape.405
  433.6 0.0 all-reduce.3.cloned.1.call-update
  433.6 0.0 all-gather.2.cloned.1.call-start
  433.7 0.0 copy-done.3
  433.7 0.6 dynamic-slice
  435.0 77.2 %all-reduce.3.cloned.1.call-done = f32[32,2,2048]{2,0,1:T(8,128)} async-done(((f32[32,2,2048]{2,0,1:T(8,128)}), f32[32,2,2048]{2,0,1:T(8,128)}) %all-reduce.3.cloned.1.call-update) | async-done | bytes 524304
  512.2 0.0 copy-done.2
  512.2 0.9 fusion.38
  513.1 0.6 copy.35
  513.8 0.0 all-gather.2.cloned.1.call-update
  513.8 719.6 %all-gather.2.cloned.1.call-done = bf16[1024,2,2048]{2,1,0:T(2,128)(2,1)} async-done(((bf16[4,2,2048]{2,1,0:T(2,128)(2,1)}), bf16[1024,2,2048]{2,1,0:T(2,128)(2,1)}) %all-gather.2.cloned.1.call-update) | async-done | bytes 8388624 | tf_op jit(solution)/shard_map/all_gather | solution.py:62
  1233.5 10.5 copy.80
  1244.0 5.3 slice_negate_fusion
  1249.2 6.2 maximum_bitcast_fusion.2
  1255.4 15.3 %fusion.27 = bf16[32,2,16,1024]{3,0,2,1:T(8,128)(2,1)S(1)} fusion(bf16[32,2,16,2048]{3,2,1,0:T(8,128)(2,1)} %param.6, bf16[1,1024,2,2048]{3,1,2,0:T(8,128)(2,1)} %maximum_bitcast_fusion.2, bf16[1,1024,2,2048]{3,1,2,0:T(8,128)(2,1)} %bitcast.118), kind=kOutput, calls=%fused_computation.34 | convolution fusion | flops 8625586176 | bytes 23068672 | tf_op jit(solution)/shard_map/vpcg,qnpg->vqcn/dot_general | solution.py:64
  1270.7 8.7 copy.40
  1279.4 20.0 %copy.41 = bf16[32,2,16,32,8,4]{3,2,5,4,1,0:T(8,128)(2,1)} copy(bf16[32,2,16,32,8,4]{0,2,5,3,4,1:T(8,128)(2,1)} %bitcast.116) | data formatting | bytes 4194304 | tf_op jit(solution)/shard_map/transpose | solution.py:67
  1299.4 17.5 %copy.42 = bf16[32,2,16,2,32,16]{0,5,4,3,2,1:T(8,128)(2,1)} copy(bf16[32,2,16,2,32,16]{4,2,5,3,1,0:T(8,128)(2,1)} %bitcast.119) | data formatting | bytes 4194304 | tf_op jit(solution)/shard_map/transpose | solution.py:69
  1316.9 10.1 copy.43
  (5 shorter events, 0.0 us)
Async XLA Ops:
  6.5 505.7 %all-reduce.3.cloned.1.call-start = ((), (), s32[]{:S(2)}) async-start(), calls=%async_computation.1 | async-start | bytes 1048576
  332.7 40.6 %copy-start = (f32[16,12,96,96]{3,2,0,1:T(8,128)S(1)}, f32[16,12,96,96]{3,2,0,1:T(8,128)}, u32[]{:S(2)}) copy-start(f32[16,12,96,96]{3,2,0,1:T(8,128)} %reshape.412) | copy-start | bytes 21233668
  332.8 40.6 %copy-start.1 = (f32[16,12,96,96]{3,2,0,1:T(8,128)S(1)}, f32[16,12,96,96]{3,2,0,1:T(8,128)}, u32[]{:S(2)}) copy-start(f32[16,12,96,96]{3,2,0,1:T(8,128)} %reshape.410) | copy-start | bytes 21233668
  424.4 9.3 copy-start.3
  424.4 87.8 %copy-start.2 = (f32[2048]{0:T(1024)S(1)}, f32[2048]{0:T(1024)}, u32[]{:S(2)}) copy-start(f32[2048]{0:T(1024)} %param.7) | copy-start | bytes 24580
  433.6 799.8 %all-gather.2.cloned.1.call-start = ((), (), s32[]{:S(2)}) async-start(), calls=%async_computation | async-start | bytes 8421376 | tf_op jit(solution)/shard_map/all_gather | solution.py:62
Sparse Core Ops, SparseCore 0:
  433.7 78.4 all-reduce.2
  514.2 719.1 all-gather.1
where the time goes:
time: 1340 us; the launch traced here: 1330 us
  waiting for transfers between devices  797 us (59%)
  blocking collectives  271 us (20%)
  local copies, waits for them, and re-layouts  121 us (9%)
  matrix products  108 us (8%)
  other arithmetic  22.6 us (2%)
  between operations  14.4 us (1%)
    all_gather x1, waiting for transfers between devices, per_device(): block_rows = lax.all_gather(scaled, ('val', 'cond'), axis=0, tiled=True)  720 us
    all_gather x1, blocking collectives, per_device(): planes = lax.all_gather(valence, 'cond', axis=3, tiled=True)  271 us
    unnamed x3, waiting for transfers between devices  77.3 us
    dot_general x1, matrix products, per_device(): jnp.einsum('vcxyz,zqk->qvcxyk', dens_imag, z_weights[1], precision=highest)  40.6 us
    dot_general x1, matrix products, per_device(): jnp.einsum('vcxyz,zqk->qvcxyk', dens_real, z_weights[0], precision=highest)  38.3 us
    transpose x2, local copies, waits for them, and re-layouts, per_device(): kernel = jnp.transpose(kernel, (0, 1, 2, 4, 3, 5))  37.5 us
  transfers between devices with their start and end apart: 2, of which 2 were waited for; matrix products, arithmetic and copies ran while one was open for 0% of the time, Pallas kernels for 0%

commit v1 on v0

v1 whole, which is shorter than its diff:
```python
import functools
import math

import jax
import jax.numpy as jnp
import ml_dtypes
import numpy as np
from jax import lax
from jax.experimental import pallas as pl
from jax.experimental.pallas import tpu as pltpu
from jax.sharding import PartitionSpec as P

GRID = 96
KXY = 16
KZ = 8
NG = 2048
NZ, NX, NY, NK = 8, 4, 4, 2
CHUNK = 1152
ROWS = 384
F32 = jnp.float32
BF16 = jnp.bfloat16


def split_bf16(a):
    hi = a.astype(ml_dtypes.bfloat16)
    lo = (a - hi.astype(np.float64)).astype(ml_dtypes.bfloat16)
    return hi, lo


@functools.lru_cache(None)
def tables():
    turn = 2.0 * math.pi / GRID
    ky = np.arange(KXY) - KXY // 2
    kz = np.arange(KZ) - KZ // 2
    angle = turn * np.mod(
        np.arange(12)[:, None, None, None] * ky[:, None] + np.arange(GRID)[:, None, None] * kz, GRID
    )
    angle = angle.reshape(CHUNK, KXY * KZ)
    c, s = np.cos(angle), np.sin(angle)
    weights = np.concatenate([np.concatenate([c, -s], 1), np.concatenate([s, c], 1)], 0)
    chunk = np.arange(8)[:, None] * np.repeat(ky, KZ)[None, :] * turn * 12
    chunk_phase = np.stack([np.cos(chunk), np.sin(chunk)], 1).astype(np.float32)
    pair = np.zeros(ROWS, np.int64)
    plane = np.zeros(ROWS, np.int64)
    for w in range(2):
        for quad in range(4):
            for i in range(4):
                base = w * 192 + quad * 48
                p = w * 16 + quad * 4 + i
                pair[base + i * 8 : base + i * 8 + 8] = p
                plane[base + i * 8 : base + i * 8 + 8] = np.arange(8)
                pair[base + 32 + i * 4 : base + 36 + i * 4] = p
                plane[base + 32 + i * 4 : base + 36 + i * 4] = 8 + np.arange(4)
    same = (np.arange(32)[:, None] == pair[None, :]).astype(np.float64)
    kx = np.arange(KXY) - KXY // 2
    ang = turn * np.mod(kx[:, None] * plane[None, :], GRID)
    cx, sx = np.cos(ang)[:, None, :] * same, np.sin(ang)[:, None, :] * same
    planes = np.stack([np.concatenate([cx, sx], 2), np.concatenate([-sx, cx], 2)], 1)
    hi, lo = split_bf16(planes.reshape(KXY * 2 * 32, 2 * ROWS))
    group = np.arange(8)[:, None] * kx[None, :] * turn * 12
    group_phase = np.stack([np.cos(group), np.sin(group)], 1).astype(np.float32)
    group_phase = np.repeat(group_phase[..., None], 128, axis=3)
    return (
        weights.astype(ml_dtypes.bfloat16),
        chunk_phase,
        np.stack([hi, lo], 0),
        group_phase,
    )


class Copies:
    def __init__(self, send, recv):
        self.send, self.recv, self.made = send, recv, []

    def start(self, src, dst, device):
        i = len(self.made)
        copy = pltpu.make_async_remote_copy(
            src_ref=src,
            dst_ref=dst,
            send_sem=self.send.at[i],
            recv_sem=self.recv.at[i],
            device_id=device,
            device_id_type=pl.DeviceIdType.MESH,
        )
        copy.start()
        self.made.append(copy)
        return copy


N_COPIES = 160


def kernel(
    cond_hbm, val_ref, res_hbm, inter_ref, w_hbm, cph_ref, plane_hbm, gph_ref,
    out_ref,
    cond_v, w_v, plane_v, res_v, yblocks, chunks, vals, rho, spec, part, asend, arecv, gath, left, outf,
    local_sem, send_sem, recv_sem,
):
    v = lax.axis_index("val")
    c = lax.axis_index("cond")
    zh, x, y = c // 16, (c // 4) % 4, c % 4
    zl, k = v // 2, v % 2
    z = zh * 4 + zl

    def at(dz=0, dx=0, dy=0, dk=0):
        tz = (z + dz) % NZ
        return {
            "val": (tz % 4) * 2 + (k + dk) % 2,
            "cond": (tz // 4) * 16 + ((x + dx) % NX) * 4 + (y + dy) % NY,
        }

    def in_val(d):
        return {"val": (v + d) % 8, "cond": c}

    copies = Copies(send_sem, recv_sem)

    order = [(h, dx) for h in range(2) for dx in (0, 1, 3, 2)]
    where = [((zh + h) % 2, (x + dx) % NX) for h, dx in order]
    load_cond = []
    load_w = pltpu.make_async_copy(w_hbm, w_v, local_sem.at[8])
    load_w.start()
    for j, (hh, xx) in enumerate(where):
        columns = pl.ds(pl.multiple_of((hh * 4 + xx) * CHUNK, 128), CHUNK)
        load = pltpu.make_async_copy(cond_hbm.at[:, :, :, columns], cond_v.at[j], local_sem.at[j])
        load.start()
        load_cond.append(load)
    load_plane = pltpu.make_async_copy(plane_hbm, plane_v, local_sem.at[9])
    load_plane.start()
    load_res = pltpu.make_async_copy(res_hbm, res_v, local_sem.at[10])
    load_res.start()

    peers = [at(dx=d) for d in (1, 2, 3)] + [at(dy=d) for d in (1, 2, 3)]
    peers += [at(dz=d) for d in range(1, 8)]
    peers += [{"val": ((zl + d) % 4) * 2 + (k + 1) % 2, "cond": c} for d in range(4)]
    barrier = pltpu.get_barrier_semaphore()
    for peer in peers:
        pl.semaphore_signal(barrier, 1, device_id=peer, device_id_type=pl.DeviceIdType.MESH)

    block = val_ref[...].astype(F32)
    rows = [block[p, w, 0:8] for p in range(2) for w in range(2)]
    rows += [block[p, w, 8:12] for p in range(2) for w in range(2)]
    block = jnp.concatenate(rows, axis=0)
    block = jnp.concatenate([block, jnp.zeros((48, 96), F32)], axis=1)
    yblocks[0, y] = block.astype(BF16)
    pl.semaphore_wait(barrier, len(peers))

    own = yblocks.at[0, y]
    from_z = copies.start(own, yblocks.at[1, y], at(dz=4))
    along_y = [[copies.start(own, own, at(dy=d)) for d in (1, 3, 2)]]

    def assemble(h):
        for copy in along_y[h]:
            copy.wait_recv()
        pieces = [yblocks[h, i].astype(F32)[:, :288] for i in range(NY)]
        chunks[h, x] = jnp.concatenate(pieces, axis=1).astype(BF16)
        mine = chunks.at[h, x]
        return [copies.start(mine, mine, at(dx=d)) for d in (1, 3)]

    def pass_on(h, along):
        d = 1 if h == 0 else 3
        there = chunks.at[h, (x + 4 - d) % NX]
        return copies.start(there, there, at(dx=d))

    spec[...] = jnp.zeros_like(spec)

    def transform(j):
        h, _ = order[j]
        hh, xx = where[j]
        load_cond[j].wait()
        vc = chunks[h, xx].astype(F32)
        for p in range(2):
            for w in range(2):
                i = p * 2 + w
                vals[p, w, 0] = vc[i * 8 : i * 8 + 8]
                four = vc[32 + i * 4 : 36 + i * 4]
                vals[p, w, 1] = jnp.concatenate([four, four], axis=0)

        def quad_step(quad, _):
            for lo in range(0, CHUNK, 384):
                lanes = slice(lo, lo + 384)
                cr = cond_v[j, 0, pl.ds(quad * 4, 4), :, lanes].astype(F32)
                ci = cond_v[j, 1, pl.ds(quad * 4, 4), :, lanes].astype(F32)
                cra, cia = cr[:, 0:8], ci[:, 0:8]
                crb = [jnp.concatenate([cr[i, 8:12], cr[i + 1, 8:12]], axis=0) for i in (0, 2)]
                cib = [jnp.concatenate([ci[i, 8:12], ci[i + 1, 8:12]], axis=0) for i in (0, 2)]
                for w in range(2):
                    vr, vi = vals[0, w, 0, :, lanes], vals[1, w, 0, :, lanes]
                    ur, ui = vals[0, w, 1, :, lanes], vals[1, w, 1, :, lanes]
                    real = [vr * cra[i] + vi * cia[i] for i in range(4)]
                    real += [ur * crb[i] + ui * cib[i] for i in range(2)]
                    imag = [vr * cia[i] - vi * cra[i] for i in range(4)]
                    imag += [ur * cib[i] - ui * crb[i] for i in range(2)]
                    at_rows = pl.ds(pl.multiple_of(w * 192 + quad * 48, 16), 48)
                    rho[at_rows, lo : lo + 384] = jnp.concatenate(real, axis=0).astype(BF16)
                    rho[at_rows, CHUNK + lo : CHUNK + lo + 384] = jnp.concatenate(
                        imag, axis=0
                    ).astype(BF16)
            return 0

        lax.fori_loop(0, 4, quad_step, 0)
        new = jnp.dot(rho[...], w_v[...], preferred_element_type=F32)
        phase = cph_ref[hh * 4 + xx]
        co, si = phase[0:1], phase[1:2]
        nr, ni = new[:, :128], new[:, 128:]
        spec[0] += nr * co + ni * si
        spec[1] += ni * co - nr * si

    along_x = [assemble(0)]
    load_w.wait()
    from_z.wait_recv()
    theirs = yblocks.at[1, y]
    along_y.append([copies.start(theirs, theirs, at(dy=d)) for d in (1, 3, 2)])
    transform(0)
    along_x[0][0].wait_recv()
    across = [pass_on(0, along_x[0])]
    along_x.append(assemble(1))
    along_x[0][1].wait_recv()
    transform(1)
    transform(2)
    across[0].wait_recv()
    transform(3)
    transform(4)
    along_x[1][0].wait_recv()
    along_x[1][1].wait_recv()
    across.append(pass_on(1, along_x[1]))
    transform(5)
    transform(6)
    across[1].wait_recv()
    transform(7)

    load_plane.wait()
    both = jnp.concatenate([spec[0], spec[1]], axis=0)
    hi = both.astype(BF16)
    low = (both - hi.astype(F32)).astype(BF16)
    pair = jnp.concatenate([hi, low], axis=1)
    for i in range(4):
        some = slice(i * 256, i * 256 + 256)
        first = jnp.dot(plane_v[0, some, :], pair, preferred_element_type=F32)
        second = jnp.dot(plane_v[1, some, :], hi, preferred_element_type=F32)
        part[some, :] = first[:, :128] + first[:, 128:] + second
    turn = gph_ref[v]
    for i in range(KXY):
        co, si = turn[0, i : i + 1], turn[1, i : i + 1]
        pr = part[i * 64 : i * 64 + 32, :]
        pi = part[i * 64 + 32 : i * 64 + 64, :]
        there = (i % 2) * 64
        asend[i // 2, there : there + 32, :] = (pr * co + pi * si).astype(BF16)
        asend[i // 2, there + 32 : there + 64, :] = (pi * co - pr * si).astype(BF16)
    exchange = []
    for d in range(1, 8):
        exchange.append(copies.start(asend.at[(v + d) % 8], arecv.at[d], in_val(d)))

    load_res.wait()

    def arrange(r, _):
        here = pl.ds(pl.multiple_of(r * 32, 16), 32)
        row = res_v[r]
        turned = jnp.concatenate([row[1], -row[0]], axis=0)
        straight = jnp.concatenate([row[0], row[1]], axis=0)
        for i in range(KXY):
            cols = slice(i * 128, i * 128 + 128)
            to = (i % 2) * 256
            left[i // 2, here, to : to + 128] = straight[:, cols]
            left[i // 2, here, to + 128 : to + 256] = turned[:, cols]
        return 0

    lax.fori_loop(0, 32, arrange, 0)

    total = asend[v].astype(F32)
    for d, copy in enumerate(exchange):
        copy.wait_recv()
        total = total + arecv[d + 1].astype(F32)
    norm = 1.0 / math.sqrt(GRID**3)
    for i in range(2):
        scale = inter_ref[pl.ds(v * 2 + i, 1), :] * norm
        for q in range(2):
            for w in range(2):
                at_row = i * 64 + q * 32 + w * 16
                tile = total[at_row : at_row + 16] * scale
                lanes = slice((i * 2 + q) * 128, (i * 2 + q) * 128 + 128)
                gath[z, k, w, x, y, :, lanes] = tile.astype(BF16)

    every = slice(None)
    lanes_a = slice(0, 128)

    def region(w, lanes, zs=z, xs=x, ys=y):
        return gath.at[zs, k, w, xs, ys, :, lanes]

    def go(ref, **d):
        return copies.start(ref, ref, at(**d))

    to_core = {0: [], 1: []}

    def hand(w, ref):
        to_core[w].append(go(ref, dk=1))

    class Gather:
        def __init__(self, w):
            self.w = w
            cut = 384 if w == 0 else 256
            self.c1, self.c2 = slice(128, cut), slice(cut, 512)

        def one(self):
            w = self.w
            ref = region(w, slice(128, 512))
            self.first = [go(ref, dz=d) for d in (4, 3, 5, 2, 6, 1, 7)]
            ref = region(w, lanes_a)
            axis = "dx" if w == 0 else "dy"
            self.first_a = [go(ref, **{axis: d}) for d in (2, 1, 3)]

        def two(self):
            w = self.w
            for copy in self.first:
                copy.wait_recv()
            r1 = region(w, self.c1, zs=every)
            r2 = region(w, self.c2, zs=every)
            self.second = [go(r1, dx=d) for d in (2, 1, 3)]
            self.second += [go(r2, dy=d) for d in (2, 1, 3)]
            for copy in self.first_a:
                copy.wait_recv()
            if w == 0:
                ra = region(w, lanes_a, xs=every)
                self.second_a = [go(ra, dy=d) for d in (2, 1, 3)]
            else:
                ra = region(w, lanes_a, ys=every)
                self.second_a = [go(ra, dx=d) for d in (2, 1, 3)]

        def three(self):
            w = self.w
            for copy in self.second:
                copy.wait_recv()
            r1 = region(w, self.c1, zs=every, xs=every)
            r2 = region(w, self.c2, zs=every, ys=every)
            self.third = [go(r1, dy=1), go(r1, dy=3), go(r2, dx=1), go(r2, dx=3)]
            for copy in self.second_a:
                copy.wait_recv()
            ra = region(w, lanes_a, xs=every, ys=every)
            self.third_a = [go(ra, dz=1), go(ra, dz=7)]
            hand(w, r1)
            hand(w, r2)
            hand(w, ra)

        def step_a(self, n):
            w = self.w
            self.third_a[0].wait_recv()
            self.third_a[1].wait_recv()
            low, high = (z + 8 - n) % 8, (z + n) % 8
            xl, xh = (every, every) if n < 3 else (slice(0, 2), slice(2, 4))
            right = region(w, lanes_a, zs=low, xs=xl, ys=every)
            leftw = region(w, lanes_a, zs=high, xs=xh, ys=every)
            self.third_a = [go(right, dz=1), go(leftw, dz=7)]
            hand(w, region(w, lanes_a, zs=low, xs=every, ys=every))
            hand(w, region(w, lanes_a, zs=high, xs=every, ys=every))

        def last_a(self):
            w = self.w
            self.third_a[0].wait_recv()
            self.third_a[1].wait_recv()
            hand(w, region(w, lanes_a, zs=(z + 4) % 8, xs=every, ys=every))

        def four(self):
            w = self.w
            ym, yp, xm, xp = (y + 3) % 4, (y + 1) % 4, (x + 3) % 4, (x + 1) % 4
            for copy in self.third:
                copy.wait_recv()
            low, high = slice(0, 4), slice(4, 8)
            self.fourth = [
                go(region(w, self.c1, zs=low, xs=every, ys=ym), dy=1),
                go(region(w, self.c1, zs=high, xs=every, ys=yp), dy=3),
                go(region(w, self.c2, zs=low, xs=xm, ys=every), dx=1),
                go(region(w, self.c2, zs=high, xs=xp, ys=every), dx=3),
            ]
            hand(w, region(w, self.c1, zs=every, xs=every, ys=ym))
            hand(w, region(w, self.c1, zs=every, xs=every, ys=yp))
            hand(w, region(w, self.c2, zs=every, xs=xm, ys=every))
            hand(w, region(w, self.c2, zs=every, xs=xp, ys=every))

        def five(self):
            w = self.w
            for copy in self.fourth:
                copy.wait_recv()
            hand(w, region(w, self.c1, zs=every, xs=every, ys=(y + 2) % 4))
            hand(w, region(w, self.c2, zs=every, xs=(x + 2) % 4, ys=every))

    factor = 2.0 / math.sqrt(NG)

    def multiply(w):
        for copy in to_core[w]:
            copy.wait_recv()

        def block_step(i, _):
            half, m = i // 4, i % 4
            at_rows = pl.ds(pl.multiple_of(m * 256, 256), 256)
            acc = jnp.zeros((256, 256), F32)
            for owner in range(8):
                new = gath[half * 4 + owner // 2, owner % 2, w].reshape(256, 512)
                acc += lax.dot_general(
                    left[owner, at_rows, :],
                    new,
                    (((1,), (1,)), ((), ())),
                    preferred_element_type=F32,
                )
            acc = acc * factor
            for t in range(2):
                start = m * 2048 + (half * 2 + t) * 2 + w
                outf[pl.ds(start, 256, stride=8), :] = acc[:, t * 128 : t * 128 + 128]
            return 0

        lax.fori_loop(0, 8, block_step, 0)

    g0, g1 = Gather(0), Gather(1)
    g0.one()
    g1.one()
    g0.two()
    g1.two()
    g0.three()
    g1.three()
    g0.step_a(1)
    g1.step_a(1)
    g0.four()
    g0.step_a(2)
    g1.step_a(2)
    g1.four()
    g0.step_a(3)
    g1.step_a(3)
    g0.five()
    g0.last_a()
    multiply(0)
    g1.five()
    g1.last_a()
    multiply(1)

    def finish(i, _):
        some = pl.ds(pl.multiple_of(i * 512, 512), 512)
        out_ref[some, :] = outf[some, :].astype(BF16)
        return 0

    lax.fori_loop(0, 16, finish, 0)
    for copy in copies.made:
        copy.wait_send()


def per_device(conduction, valence, resident, interaction):
    weights, chunk_phase, planes, group_phase = (jnp.asarray(t) for t in tables())
    anywhere = pl.BlockSpec(memory_space=pl.ANY)
    vmem = pl.BlockSpec(memory_space=pltpu.VMEM)
    out = pl.pallas_call(
        kernel,
        name="exchange_row",
        out_shape=jax.ShapeDtypeStruct((8192, 128), BF16),
        in_specs=[anywhere, vmem, anywhere, vmem, anywhere, vmem, anywhere, vmem],
        out_specs=vmem,
        scratch_shapes=[
            pltpu.VMEM((8, 2, 16, 12, CHUNK), BF16),
            pltpu.VMEM((2 * CHUNK, 256), BF16),
            pltpu.VMEM((2, 1024, 768), BF16),
            pltpu.VMEM((32, 2, 16, NG), BF16),
            pltpu.VMEM((2, NY, 48, 384), BF16),
            pltpu.VMEM((2, NX, 48, CHUNK), BF16),
            pltpu.VMEM((2, 2, 2, 8, CHUNK), F32),
            pltpu.VMEM((ROWS, 2 * CHUNK), BF16),
            pltpu.VMEM((2, ROWS, 128), F32),
            pltpu.VMEM((1024, 128), F32),
            pltpu.VMEM((8, 128, 128), BF16),
            pltpu.VMEM((8, 128, 128), BF16),
            pltpu.VMEM((NZ, NK, 2, NX, NY, 16, 512), BF16),
            pltpu.VMEM((8, 1024, 512), BF16),
            pltpu.VMEM((8192, 128), F32),
            pltpu.SemaphoreType.DMA((11,)),
            pltpu.SemaphoreType.DMA((N_COPIES,)),
            pltpu.SemaphoreType.DMA((N_COPIES,)),
        ],
        compiler_params=pltpu.CompilerParams(
            collective_id=0, has_side_effects=True, vmem_limit_bytes=56 << 20
        ),
    )(
        conduction,
        valence,
        resident,
        interaction.reshape(KXY, 128),
        weights,
        chunk_phase,
        planes,
        group_phase,
    )
    out = out.reshape(32, 2, 16, 4, 2, 128)
    out = jnp.transpose(out, (0, 1, 2, 4, 3, 5))
    return out.reshape(32, 2, 16, 2, 512)


def solution(mesh):
    in_specs = (
        P(None, "cond", "val", None),
        P(None, None, "val", "cond"),
        P("val", None, "cond", None),
        P(),
    )
    out_specs = P("val", None, "cond", None, None)
    return jax.shard_map(
        per_device, mesh=mesh, in_specs=in_specs, out_specs=out_specs, check_vma=False
    )
```

time: 1340 us -> 103 us (0.08)
  waiting for transfers between devices: 797 us -> 0 us
  blocking collectives: 271 us -> 0 us
  matrix products: 108 us -> 0 us
  local copies, waits for them, and re-layouts: 121 us -> 18.1 us
  Pallas kernels: 0 us -> 84.9 us
  other arithmetic: 22.6 us -> 0 us
  between operations: 14.4 us -> 0.01 us
    all_gather x1 -> x0, waiting for transfers between devices: 720 us -> none  [per_device(): block_rows = lax.all_gather(scaled, ('val', 'cond'), axis=0, tiled=True)]
    all_gather x1 -> x0, blocking collectives: 271 us -> none  [per_device(): planes = lax.all_gather(valence, 'cond', axis=3, tiled=True)]
    dot_general x5 -> x0, matrix products: 108 us -> none  [the longest x1 40.6 us: per_device(): jnp.einsum('vcxyz,zqk->qvcxyk', dens_imag, z_weights[1], precision=highest)]
    pallas_call x0 -> x1, Pallas kernels: none -> 84.9 us  [per_device(): pl.pallas_call(kernel, name='exchange_row', out_shape=jax.ShapeDtypeStruc...]
    unnamed x3 -> x0, waiting for transfers between devices: 77.3 us -> none
    convert_element_type x6 -> x0, local copies, waits for them, and re-layouts: 45.6 us -> none  [the longest x1 9.35 us: per_device(): conduction[1].astype(jnp.float32)]
    transpose x3 -> x0, local copies, waits for them, and re-layouts: 40 us -> none  [the longest x2 37.5 us: per_device(): kernel = jnp.transpose(kernel, (0, 1, 2, 4, 3, 5))]
    unnamed x10 -> x3, local copies, waits for them, and re-layouts: 1.65 us -> 18.1 us
  transfers between devices with their start and end apart: 2 -> 0, of which waited for: 2 -> 0; matrix products, arithmetic and copies ran while one was open for 0% -> 0% of each run, Pallas kernels for 0% -> 0%
where the time goes in v1:
time: 103 us
  Pallas kernels  84.9 us (82%)
  local copies, waits for them, and re-layouts  18.1 us (18%)
    pallas_call x1, Pallas kernels, per_device(): pl.pallas_call(kernel, name='exchange_row', out_shape=jax.ShapeDtypeStruc...  84.9 us
    unnamed x3, local copies, waits for them, and re-layouts  18.1 us

profile of v1, /device:TPU:1, one launch (start us, length us, event | category | flops | bytes accessed | tf_op | source)
XLA Modules:
  0.0 103.0 jit_solution(17818379057164655736)
XLA Ops:
  0.0 1.4 %copy.10.val_ref = bf16[2,2,12,288]{3,2,1,0:T(8,128)(2,1)} copy(bf16[2,2,12,288]{3,1,2,0:T(2,128)(2,1)} %param.9) | data formatting | bytes 55296 | tf_op args[1]
  1.4 10.7 %copy.9.cond_hbm = bf16[2,16,12,9216]{3,2,1,0:T(8,128)(2,1)} copy(bf16[2,16,12,9216]{3,1,2,0:T(8,128)(2,1)} %param.8) | data formatting | bytes 14155776 | tf_op args[0]
  12.1 84.9 %exchange_row.1 = bf16[8192,128]{1,0:T(8,128)(2,1)} custom-call(bf16[2,16,12,9216]{3,2,1,0:T(8,128)(2,1)} %copy.9.cond_hbm, bf16[2,2,12,288]{3,2,1,0:T(8,128)(2,1)} %copy.10.val_ref, bf16[32,2,16,2048]{3,2,1,0:T(8,128)(2,1)} %res_hbm.1, f32[16,128]{1,0:T(8,128)} %bitcast.7, bf16[2304,256]{1,0:T(8,128)(2,1)} %constant.8.clone.w_hbm, ...), custom_call_target="tpu_custom_call" | custom-call | tf_op jit(solution)/shard_map/exchange_row/pallas_call | solution.py:447
  97.0 6.0 %copy.13 = bf16[32,2,16,2,512]{4,3,2,1,0:T(2,128)(2,1)} copy(bf16[32,2,16,2,512]{4,3,2,1,0:T(2,128)(2,1)} %bitcast.6) | data formatting | bytes 4194304

commit v2 on v1

v2 whole, which is shorter than its diff:
```python
import functools
import math

import jax
import jax.numpy as jnp
import ml_dtypes
import numpy as np
from jax import lax
from jax.experimental import pallas as pl
from jax.experimental.pallas import tpu as pltpu
from jax.sharding import PartitionSpec as P

GRID = 96
KXY = 16
KZ = 8
NG = 2048
NZ, NX, NY, NK = 8, 4, 4, 2
CHUNK = 1152
ROWS = 384
F32 = jnp.float32
BF16 = jnp.bfloat16


def split_bf16(a):
    hi = a.astype(ml_dtypes.bfloat16)
    lo = (a - hi.astype(np.float64)).astype(ml_dtypes.bfloat16)
    return hi, lo


@functools.lru_cache(None)
def tables():
    turn = 2.0 * math.pi / GRID
    ky = np.arange(KXY) - KXY // 2
    kz = np.arange(KZ) - KZ // 2
    angle = turn * np.mod(
        np.arange(12)[:, None, None, None] * ky[:, None] + np.arange(GRID)[:, None, None] * kz, GRID
    )
    angle = angle.reshape(CHUNK, KXY * KZ)
    c, s = np.cos(angle), np.sin(angle)
    weights = np.concatenate([np.concatenate([c, -s], 1), np.concatenate([s, c], 1)], 0)
    chunk = np.arange(8)[:, None] * np.repeat(ky, KZ)[None, :] * turn * 12
    chunk_phase = np.stack([np.cos(chunk), np.sin(chunk)], 1).astype(np.float32)
    row = np.arange(ROWS)
    pair, plane = row // 192 * 16 + row % 16, row % 192 // 16
    same = (np.arange(32)[:, None] == pair[None, :]).astype(np.float64)
    kx = np.arange(KXY) - KXY // 2
    ang = turn * np.mod(kx[:, None] * plane[None, :], GRID)
    cx, sx = np.cos(ang)[:, None, :] * same, np.sin(ang)[:, None, :] * same
    planes = np.stack([np.concatenate([cx, sx], 2), np.concatenate([-sx, cx], 2)], 1)
    hi, lo = split_bf16(planes.reshape(KXY * 2 * 32, 2 * ROWS))
    group = np.arange(8)[:, None] * kx[None, :] * turn * 12
    group_phase = np.stack([np.cos(group), np.sin(group)], 1).astype(np.float32)
    group_phase = np.repeat(group_phase[..., None], 128, axis=3)
    return (
        weights.astype(ml_dtypes.bfloat16),
        chunk_phase,
        np.stack([hi, lo], 0),
        group_phase,
    )


class Group:
    def __init__(self, send, recv, total, device):
        self.send, self.recv, self.device = send, recv, device
        self.whole = self.describe(total, total, device)

    def describe(self, src, dst, device):
        return pltpu.make_async_remote_copy(
            src_ref=src,
            dst_ref=dst,
            send_sem=self.send,
            recv_sem=self.recv,
            device_id=device,
            device_id_type=pl.DeviceIdType.MESH,
        )

    def start(self, src, dst, device):
        self.describe(src, dst, device).start()

    def wait_recv(self):
        self.whole.wait_recv()

    def wait_send(self):
        self.whole.wait_send()


class Copies:
    def __init__(self, send, recv, device):
        self.send, self.recv, self.device, self.made = send, recv, device, []

    def group(self, total):
        i = len(self.made)
        made = Group(self.send.at[i], self.recv.at[i], total, self.device)
        self.made.append(made)
        return made

    def start(self, src, dst, device):
        made = self.group(src)
        made.start(src, dst, device)
        return made


N_GROUPS = 56


def kernel(
    cond_hbm, val_hbm, res_hbm, inter_hbm, w_hbm, cph_hbm, plane_hbm, gph_hbm,
    out_ref,
    val_ref, inter_ref, cph_ref, gph_ref, cond_v, w_v, plane_v, res_v, yblocks, chunks, vals, rho, spec, part, asend, arecv, gath, left, acc, outf,
    local_sem, send_sem, recv_sem,
):
    v = lax.axis_index("val")
    c = lax.axis_index("cond")
    zh, x, y = c // 16, (c // 4) % 4, c % 4
    zl, k = v // 2, v % 2
    z = zh * 4 + zl

    def at(dz=0, dx=0, dy=0, dk=0):
        tz = (z + dz) % NZ
        return {
            "val": (tz % 4) * 2 + (k + dk) % 2,
            "cond": (tz // 4) * 16 + ((x + dx) % NX) * 4 + (y + dy) % NY,
        }

    def in_val(d):
        return {"val": (v + d) % 8, "cond": c}

    copies = Copies(send_sem, recv_sem, at(dk=1))

    def chunk_at(j):
        i = j % 4
        return j // 4, (x + i + i // 2 - 2 * (i // 3)) % NX

    def load_chunk(j):
        h, xx = chunk_at(j)
        columns = pl.ds(pl.multiple_of(((zh + h) % 2 * 4 + xx) * CHUNK, 128), CHUNK)
        return pltpu.make_async_copy(
            cond_hbm.at[:, :, :, columns], cond_v.at[j], local_sem.at[j]
        )

    load_val = pltpu.make_async_copy(val_hbm, val_ref, local_sem.at[11])
    load_val.start()
    small = [(cph_hbm, cph_ref), (gph_hbm.at[v], gph_ref), (inter_hbm, inter_ref)]
    load_small = [
        pltpu.make_async_copy(src, dst, local_sem.at[12 + i]) for i, (src, dst) in enumerate(small)
    ]
    for load in load_small:
        load.start()
    load_w = pltpu.make_async_copy(w_hbm, w_v, local_sem.at[8])
    load_w.start()
    for j in range(8):
        load_chunk(j).start()
    load_plane = pltpu.make_async_copy(plane_hbm, plane_v, local_sem.at[9])
    load_plane.start()
    load_res = pltpu.make_async_copy(res_hbm, res_v, local_sem.at[10])
    load_res.start()

    plane_peers = [(i, j) for i in (2, 1, 3, 0) for j in (2, 1, 3, 0) if i or j]
    peers = [at(dx=i, dy=j) for i, j in plane_peers]
    peers += [at(dz=d) for d in range(1, 8)]
    peers += [{"val": ((zl + d) % 4) * 2 + (k + 1) % 2, "cond": c} for d in range(4)]
    barrier = pltpu.get_barrier_semaphore()
    for peer in peers:
        pl.semaphore_signal(barrier, 1, device_id=peer, device_id_type=pl.DeviceIdType.MESH)

    load_val.wait()
    block = val_ref[...].astype(F32).reshape(48, 288)
    block = jnp.concatenate([block, jnp.zeros((48, 96), F32)], axis=1)
    yblocks[0, y] = block.astype(BF16)
    pl.semaphore_wait(barrier, len(peers))

    own = yblocks.at[0, y]
    from_z = copies.start(own, yblocks.at[1, y], at(dz=4))
    along_y = [[copies.start(own, own, at(dy=d)) for d in (1, 3, 2)]]

    def assemble(h):
        for copy in along_y[h]:
            copy.wait_recv()
        pieces = [yblocks[h, i].astype(F32)[:, :288] for i in range(NY)]
        chunks[h, x] = jnp.concatenate(pieces, axis=1).astype(BF16)

    one_chunk = chunks.at[0, 0]
    near = {d: copies.group(one_chunk) for d in (1, 3)}
    across = copies.group(one_chunk)
    far = {d: copies.group(one_chunk) for d in (2, 1, 3)}

    spec[...] = jnp.zeros_like(spec)
    acc[...] = jnp.zeros_like(acc)

    def transform(j):
        h, xx = chunk_at(j)
        load_chunk(j).wait()
        vals[...] = chunks[h, xx].astype(F32)

        def plane_step(plane, _):
            at_rows = [pl.ds(pl.multiple_of(w * 192 + plane * 16, 16), 16) for w in range(2)]
            for lo in range(0, CHUNK, 384):
                lanes = slice(lo, lo + 384)
                cr = cond_v[j, 0, plane, :, lanes].astype(F32)
                ci = cond_v[j, 1, plane, :, lanes].astype(F32)
                for w in range(2):
                    vr = vals[pl.ds(plane * 2 + w, 1), lanes]
                    vi = vals[pl.ds(24 + plane * 2 + w, 1), lanes]
                    rho[at_rows[w], lo : lo + 384] = (vr * cr + vi * ci).astype(BF16)
                    rho[at_rows[w], CHUNK + lo : CHUNK + lo + 384] = (vr * ci - vi * cr).astype(BF16)
            return 0

        lax.fori_loop(0, 12, plane_step, 0)
        new = jnp.dot(rho[...], w_v[...], preferred_element_type=F32)
        phase = cph_ref[(zh + h) % 2 * 4 + xx]
        co, si = phase[0:1], phase[1:2]
        nr, ni = new[:, :128], new[:, 128:]
        spec[0] += nr * co + ni * si
        spec[1] += ni * co - nr * si

    assemble(0)
    mine = chunks.at[0, x]
    for d, group in near.items():
        group.start(mine, mine, at(dx=d))
    from_z.wait_recv()
    theirs = yblocks.at[1, y]
    along_y.append([copies.start(theirs, theirs, at(dy=d)) for d in (1, 3, 2)])
    load_w.wait()
    for load in load_small:
        load.wait()

    def chunk_step(j, _):
        @pl.when(j == 1)
        def _():
            near[1].wait_recv()
            passed = chunks.at[0, (x + 3) % NX]
            across.start(passed, passed, at(dx=1))
            assemble(1)
            partners = chunks.at[1, x]
            for d, group in far.items():
                group.start(partners, partners, at(dx=d))
            near[3].wait_recv()

        for place, group in ((3, across), (5, far[3]), (6, far[1]), (7, far[2])):
            pl.when(j == place)(group.wait_recv)
        transform(j)
        return 0

    lax.fori_loop(0, 8, chunk_step, 0)

    load_plane.wait()
    both = jnp.concatenate([spec[0], spec[1]], axis=0)
    hi = both.astype(BF16)
    low = (both - hi.astype(F32)).astype(BF16)
    pair = jnp.concatenate([hi, low], axis=1)

    def plane_rows(i, _):
        some = pl.ds(pl.multiple_of(i * 256, 256), 256)
        first = jnp.dot(plane_v[0, some, :], pair, preferred_element_type=F32)
        second = jnp.dot(plane_v[1, some, :], hi, preferred_element_type=F32)
        part[some, :] = first[:, :128] + first[:, 128:] + second
        return 0

    lax.fori_loop(0, 4, plane_rows, 0)
    turn = gph_ref[...]
    for i in range(KXY):
        co, si = turn[0, i : i + 1], turn[1, i : i + 1]
        pr = part[i * 64 : i * 64 + 32, :]
        pi = part[i * 64 + 32 : i * 64 + 64, :]
        there = (i % 2) * 64
        asend[i // 2, there : there + 32, :] = (pr * co + pi * si).astype(BF16)
        asend[i // 2, there + 32 : there + 64, :] = (pi * co - pr * si).astype(BF16)
    exchange = copies.group(arecv.at[1:8])
    for d in range(1, 8):
        exchange.start(asend.at[(v + d) % 8], arecv.at[d], in_val(d))

    load_res.wait()

    def arrange(r, _):
        here = pl.ds(pl.multiple_of(r * 32, 16), 32)
        row = res_v[r]
        turned = jnp.concatenate([row[1], -row[0]], axis=0)
        straight = jnp.concatenate([row[0], row[1]], axis=0)
        for i in range(KXY):
            cols = slice(i * 128, i * 128 + 128)
            to = (i % 2) * 256
            left[i // 2, here, to : to + 128] = straight[:, cols]
            left[i // 2, here, to + 128 : to + 256] = turned[:, cols]
        return 0

    lax.fori_loop(0, 32, arrange, 0)

    total = asend[v].astype(F32)
    exchange.wait_recv()
    for d in range(1, 8):
        total = total + arecv[d].astype(F32)
    norm = 1.0 / math.sqrt(GRID**3)
    for i in range(2):
        scale = inter_ref[pl.ds(v * 2 + i, 1), :] * norm
        for q in range(2):
            for w in range(2):
                at_row = i * 64 + q * 32 + w * 16
                tile = total[at_row : at_row + 16] * scale
                lanes = slice((i * 2 + q) * 128, (i * 2 + q) * 128 + 128)
                gath[z, k, w, x, y, :, lanes] = tile.astype(BF16)

    every = slice(None)
    lanes_a = slice(0, 128)
    cuts = (384, 256)

    def region(w, lanes, zs, xs, ys):
        return gath.at[zs, k, w, xs, ys, :, lanes]

    def go(group, ref, **d):
        group.start(ref, ref, at(**d))

    def wait_all(some):
        for group in some:
            group.wait_recv()

    def lanes_c(w):
        return slice(128, cuts[w]), slice(cuts[w], 512)

    lanes_both = slice(128, 512)
    halves = (slice(0, 4), slice(4, 8))
    near_two, near_three = slice(0, 2), slice(0, 3)
    hand_a = [copies.group(region(w, lanes_a, every, every, every)) for w in range(2)]
    hand_c = [
        [copies.group(region(w, lanes_both, zs, every, every)) for zs in halves] for w in range(2)
    ]

    def first():
        sends_c = copies.group(region(every, lanes_both, slice(0, 7), x, y))
        ref = region(every, lanes_both, z, x, y)
        for d in (4, 3, 5, 2, 6, 1, 7):
            go(sends_c, ref, dz=d)
        ref = region(every, lanes_a, z, x, y)
        other = copies.group(region(every, lanes_a, z, near_three, every))
        same = copies.group(region(every, lanes_a, z, x, near_three))
        for i, j in plane_peers:
            go(other if i else same, ref, dx=i, dy=j)
        return sends_c, (other, same)

    def second():
        sends = []
        for w in range(2):
            c1, c2 = lanes_c(w)
            g1 = copies.group(region(w, c1, every, near_three, y))
            g2 = copies.group(region(w, c2, every, x, near_three))
            for d in (2, 1, 3):
                go(g1, region(w, c1, every, x, y), dx=d)
                go(g2, region(w, c2, every, x, y), dy=d)
            sends += [g1, g2]
        return sends

    def hand_second():
        for w in range(2):
            c1, c2 = lanes_c(w)
            for h, zs in enumerate(halves):
                go(hand_c[w][h], region(w, c1, zs, every, y), dk=1)
                go(hand_c[w][h], region(w, c2, zs, x, every), dk=1)

    def along_z(n, before):
        after = []
        for w in range(2):
            if n > 1:
                before[w].wait_recv()
            zs, xl, xh = (near_two, every, every) if n < 4 else (0, slice(0, 2), slice(2, 4))
            low, high = (z + 9 - n) % NZ, (z + n - 1) % NZ
            group = copies.group(region(w, lanes_a, zs, every, every))
            go(group, region(w, lanes_a, low, xl, every), dz=1)
            go(group, region(w, lanes_a, high, xh, every), dz=7)
            after.append(group)
            go(hand_a[w], region(w, lanes_a, low, every, every), dk=1)
            if n > 1:
                go(hand_a[w], region(w, lanes_a, high, every, every), dk=1)
        return after

    def end_z(before):
        for w in range(2):
            before[w].wait_recv()
            go(hand_a[w], region(w, lanes_a, (z + 4) % NZ, every, every), dk=1)

    def third(w, h):
        zs = halves[h]
        c1, c2 = lanes_c(w)
        g1 = copies.group(region(w, c1, zs, every, near_two))
        g2 = copies.group(region(w, c2, zs, near_two, every))
        for d in (1, 3):
            go(g1, region(w, c1, zs, every, y), dy=d)
            go(g2, region(w, c2, zs, x, every), dx=d)
        return g1, g2

    def fourth(w, h, before):
        wait_all(before)
        zs = halves[h]
        c1, c2 = lanes_c(w)
        low, high = slice(h * 4, h * 4 + 2), slice(h * 4 + 2, h * 4 + 4)
        ym, yp, xm, xp = (y + 3) % NY, (y + 1) % NY, (x + 3) % NX, (x + 1) % NX
        g1 = copies.group(region(w, c1, zs, every, 0))
        g2 = copies.group(region(w, c2, zs, 0, every))
        go(g1, region(w, c1, low, every, ym), dy=1)
        go(g1, region(w, c1, high, every, yp), dy=3)
        go(g2, region(w, c2, low, xm, every), dx=1)
        go(g2, region(w, c2, high, xp, every), dx=3)
        for i in (ym, yp):
            go(hand_c[w][h], region(w, c1, zs, every, i), dk=1)
        for i in (xm, xp):
            go(hand_c[w][h], region(w, c2, zs, i, every), dk=1)
        return g1, g2

    def fifth(w, h, before):
        wait_all(before)
        zs = halves[h]
        c1, c2 = lanes_c(w)
        go(hand_c[w][h], region(w, c1, zs, every, (y + 2) % NY), dk=1)
        go(hand_c[w][h], region(w, c2, zs, (x + 2) % NX, every), dk=1)

    factor = 2.0 / math.sqrt(NG)

    def multiply(w, h, lanes, planes):
        def step(i, _):
            owners = [(i * planes + j, q) for j in range(planes) for q in range(NK)]
            rows = jnp.concatenate([left[j * NK + q, :, lanes] for j, q in owners], axis=1)
            new = [gath[h * 4 + j, q, w, :, :, :, lanes].reshape(256, -1) for j, q in owners]
            acc[w, h] += lax.dot_general(
                rows,
                jnp.concatenate(new, axis=1),
                (((1,), (1,)), ((), ())),
                preferred_element_type=F32,
            )
            return 0

        lax.fori_loop(0, 4 // planes, step, 0)

    def store(w, h):
        def block_step(m, _):
            at_rows = pl.ds(pl.multiple_of(m * 128, 128), 128)
            for t in range(2):
                start = m * 1024 + (h * 2 + t) * 2 + w
                tile = acc[w, h, at_rows, t * 128 : t * 128 + 128] * factor
                outf[pl.ds(start, 128, stride=8), :] = tile
            return 0

        lax.fori_loop(0, 8, block_step, 0)

    sends_c, sends_a = first()
    wait_all(sends_a)
    steps_a = along_z(1, None)
    sends_c.wait_recv()
    sends_c = second()
    steps_a = along_z(2, steps_a)
    wait_all(sends_c)
    p0, p1, p2 = third(0, 0), third(0, 1), third(1, 0)
    hand_second()
    steps_a = along_z(3, steps_a)
    p0 = fourth(0, 0, p0)
    p3 = third(1, 1)
    p1 = fourth(0, 1, p1)
    steps_a = along_z(4, steps_a)
    p2 = fourth(1, 0, p2)
    fifth(0, 0, p0)
    p3 = fourth(1, 1, p3)
    fifth(0, 1, p1)

    def products(s, _):
        w, h = s // 2, s % 2

        @pl.when(s == 0)
        def _():
            hand_c[0][0].wait_recv()

        @pl.when(s == 1)
        def _():
            fifth(1, 0, p2)
            hand_c[0][1].wait_recv()

        @pl.when(s == 2)
        def _():
            hand_c[1][0].wait_recv()
            hand_a[1].wait_recv()

        @pl.when(s == 3)
        def _():
            hand_c[1][1].wait_recv()

        multiply(w, h, lanes_both, 1)

        @pl.when(s == 0)
        def _():
            end_z(steps_a)
            hand_a[0].wait_recv()

        @pl.when(s == 1)
        def _():
            fifth(1, 1, p3)

        multiply(w, h, lanes_a, 2)
        store(w, h)
        return 0

    lax.fori_loop(0, 4, products, 0)

    def finish(m, _):
        some = pl.ds(pl.multiple_of(m * 1024, 1024), 1024)
        out_ref[some, :] = outf[some, :].astype(BF16)
        return 0

    lax.fori_loop(0, 8, finish, 0)
    for copy in copies.made:
        copy.wait_send()


def write_out(in_ref, out_ref, buf, in_sem, out_sem):
    pieces = [pl.ds(i * 2048, 2048) for i in range(4)]
    loads = [
        pltpu.make_async_copy(in_ref.at[p], buf.at[i], in_sem.at[i]) for i, p in enumerate(pieces)
    ]
    stores = [
        pltpu.make_async_copy(buf.at[i], out_ref.at[p], out_sem.at[i]) for i, p in enumerate(pieces)
    ]
    for load in loads:
        load.start()
    for load, store in zip(loads, stores):
        load.wait()
        store.start()
    for store in stores:
        store.wait()


def per_device(conduction, valence, resident, interaction):
    weights, chunk_phase, planes, group_phase = (jnp.asarray(t) for t in tables())
    anywhere = pl.BlockSpec(memory_space=pl.ANY)
    vmem = pl.BlockSpec(memory_space=pltpu.VMEM)
    out = pl.pallas_call(
        kernel,
        name="exchange_row",
        out_shape=jax.ShapeDtypeStruct((8192, 128), BF16),
        in_specs=[anywhere] * 8,
        out_specs=vmem,
        scratch_shapes=[
            pltpu.VMEM((2, 12, 2, 288), BF16),
            pltpu.VMEM((KXY, 128), F32),
            pltpu.VMEM((8, 2, 128), F32),
            pltpu.VMEM((2, KXY, 128), F32),
            pltpu.VMEM((8, 2, 12, 16, CHUNK), BF16),
            pltpu.VMEM((2 * CHUNK, 256), BF16),
            pltpu.VMEM((2, 1024, 768), BF16),
            pltpu.VMEM((32, 2, 16, NG), BF16),
            pltpu.VMEM((2, NY, 48, 384), BF16),
            pltpu.VMEM((2, NX, 48, CHUNK), BF16),
            pltpu.VMEM((48, CHUNK), F32),
            pltpu.VMEM((ROWS, 2 * CHUNK), BF16),
            pltpu.VMEM((2, ROWS, 128), F32),
            pltpu.VMEM((1024, 128), F32),
            pltpu.VMEM((8, 128, 128), BF16),
            pltpu.VMEM((8, 128, 128), BF16),
            pltpu.VMEM((NZ, NK, 2, NX, NY, 16, 512), BF16),
            pltpu.VMEM((8, 1024, 512), BF16),
            pltpu.VMEM((2, 2, 1024, 256), F32),
            pltpu.VMEM((8192, 128), F32),
            pltpu.SemaphoreType.DMA((15,)),
            pltpu.SemaphoreType.DMA((N_GROUPS,)),
            pltpu.SemaphoreType.DMA((N_GROUPS,)),
        ],
        compiler_params=pltpu.CompilerParams(
            collective_id=0, has_side_effects=True, vmem_limit_bytes=56 << 20
        ),
    )(
        jnp.transpose(conduction, (0, 2, 1, 3)),
        jnp.transpose(valence, (0, 2, 1, 3)),
        resident,
        interaction.reshape(KXY, 128),
        weights,
        chunk_phase,
        planes,
        group_phase,
    )
    out = pl.pallas_call(
        write_out,
        name="write_out",
        out_shape=jax.ShapeDtypeStruct((8192, 128), BF16),
        in_specs=[anywhere],
        out_specs=anywhere,
        scratch_shapes=[
            pltpu.VMEM((4, 2048, 128), BF16),
            pltpu.SemaphoreType.DMA((4,)),
            pltpu.SemaphoreType.DMA((4,)),
        ],
    )(out)
    out = out.reshape(32, 2, 16, 4, 2, 128)
    out = jnp.transpose(out, (0, 1, 2, 4, 3, 5))
    return out.reshape(32, 2, 16, 2, 512)


def solution(mesh):
    in_specs = (
        P(None, "cond", "val", None),
        P(None, None, "val", "cond"),
        P("val", None, "cond", None),
        P(),
    )
    out_specs = P("val", None, "cond", None, None)
    return jax.shard_map(
        per_device, mesh=mesh, in_specs=in_specs, out_specs=out_specs, check_vma=False
    )
```

time: 103 us -> 87.7 us (0.85)
  local copies, waits for them, and re-layouts: 18.1 us -> 0 us
  Pallas kernels: 84.9 us -> 87.6 us
    unnamed x3 -> x0, local copies, waits for them, and re-layouts: 18.1 us -> none
    pallas_call x0 -> x1, Pallas kernels: none -> 2.42 us  [per_device(): pl.pallas_call(write_out, name='write_out', out_shape=jax.ShapeDtypeStruc...]
where the time goes in v2:
time: 87.7 us; the launch traced here: 87.6 us
  Pallas kernels  87.6 us (100%)
    pallas_call x1, Pallas kernels, per_device(): pl.pallas_call(kernel, name='exchange_row', out_shape=jax.ShapeDtypeStruc...  85.2 us
    pallas_call x1, Pallas kernels, per_device(): pl.pallas_call(write_out, name='write_out', out_shape=jax.ShapeDtypeStruc...  2.42 us

profile of v2, /device:TPU:1, one launch (start us, length us, event | category | flops | bytes accessed | tf_op | source)
XLA Modules:
  0.0 87.6 jit_solution(18109261715557189861)
XLA Ops:
  0.0 85.2 %exchange_row.1.in_ref = bf16[8192,128]{1,0:T(8,128)(2,1)} custom-call(bf16[2,12,16,9216]{3,2,1,0:T(8,128)(2,1)} %bitcast.8, bf16[2,12,2,288]{3,2,1,0:T(2,128)(2,1)} %bitcast.9, bf16[32,2,16,2048]{3,2,1,0:T(8,128)(2,1)} %res_hbm.1, f32[16,128]{1,0:T(8,128)} %bitcast.10, bf16[2304,256]{1,0:T(8,128)(2,1)} %constant.8.clone.w_hbm, ...), custom_call_target="tpu_custom_call" | custom-call | tf_op jit(solution)/shard_map/exchange_row/pallas_call | solution.py:530
  85.2 2.4 %write_out.1 = bf16[8192,128]{1,0:T(8,128)(2,1)} custom-call(bf16[8192,128]{1,0:T(8,128)(2,1)} %exchange_row.1.in_ref), custom_call_target="tpu_custom_call" | custom-call | tf_op jit(solution)/shard_map/write_out/pallas_call | solution.py:574

commit v3 on v2

--- a/solution.py
+++ b/solution.py
@@ -105,8 +105,8 @@
 
 def kernel(
     cond_hbm, val_hbm, res_hbm, inter_hbm, w_hbm, cph_hbm, plane_hbm, gph_hbm,
-    out_ref,
-    val_ref, inter_ref, cph_ref, gph_ref, cond_v, w_v, plane_v, res_v, yblocks, chunks, vals, rho, spec, part, asend, arecv, gath, left, acc, outf,
+    out_hbm,
+    val_ref, inter_ref, cph_ref, gph_ref, cond_v, w_v, plane_v, res_v, yblocks, chunks, vals, rho, spec, part, asend, arecv, gath, left, outf, out_v,
     local_sem, send_sem, recv_sem,
 ):
     v = lax.axis_index("val")
@@ -185,7 +185,6 @@
     far = {d: copies.group(one_chunk) for d in (2, 1, 3)}
 
     spec[...] = jnp.zeros_like(spec)
-    acc[...] = jnp.zeros_like(acc)
 
     def transform(j):
         h, xx = chunk_at(j)
@@ -413,31 +412,41 @@
 
     factor = 2.0 / math.sqrt(NG)
 
-    def multiply(w, h, lanes, planes):
-        def step(i, _):
-            owners = [(i * planes + j, q) for j in range(planes) for q in range(NK)]
-            rows = jnp.concatenate([left[j * NK + q, :, lanes] for j, q in owners], axis=1)
-            new = [gath[h * 4 + j, q, w, :, :, :, lanes].reshape(256, -1) for j, q in owners]
-            acc[w, h] += lax.dot_general(
+    def multiply(s):
+        w, h = s // 2, s % 2
+        owners = [(i, q) for i in range(4) for q in range(NK)]
+
+        def rows_step(m, _):
+            at_rows = pl.ds(pl.multiple_of(m * 512, 512), 512)
+            rows = jnp.concatenate([left[i * NK + q, at_rows, :] for i, q in owners], axis=1)
+            new = [gath[h * 4 + i, q, w].reshape(256, 512) for i, q in owners]
+            product = factor * lax.dot_general(
                 rows,
                 jnp.concatenate(new, axis=1),
                 (((1,), (1,)), ((), ())),
                 preferred_element_type=F32,
             )
+            for t in range(2):
+                start = m * 4096 + (h * 2 + t) * 2 + w
+                outf[pl.ds(start, 512, stride=8), :] = product[:, t * 128 : t * 128 + 128]
+
+            @pl.when(s == 3)
+            def _():
+                def finish(i, _):
+                    some = pl.ds(pl.multiple_of(m * 4096 + i * 1024, 1024), 1024)
+                    out_v[some, :] = outf[some, :].astype(BF16)
+                    return 0
+
+                lax.fori_loop(0, 4, finish, 0)
+                write_back(m).start()
+
             return 0
 
-        lax.fori_loop(0, 4 // planes, step, 0)
-
-    def store(w, h):
-        def block_step(m, _):
-            at_rows = pl.ds(pl.multiple_of(m * 128, 128), 128)
-            for t in range(2):
-                start = m * 1024 + (h * 2 + t) * 2 + w
-                tile = acc[w, h, at_rows, t * 128 : t * 128 + 128] * factor
-                outf[pl.ds(start, 128, stride=8), :] = tile
-            return 0
-
-        lax.fori_loop(0, 8, block_step, 0)
+        lax.fori_loop(0, 2, rows_step, 0)
+
+    def write_back(m):
+        some = pl.ds(pl.multiple_of(m * 4096, 4096), 4096)
+        return pltpu.make_async_copy(out_v.at[some], out_hbm.at[some], local_sem.at[15 + m])
 
     sends_c, sends_a = first()
     wait_all(sends_a)
@@ -458,12 +467,13 @@
     p3 = fourth(1, 1, p3)
     fifth(0, 1, p1)
 
+    end_z(steps_a)
+
     def products(s, _):
-        w, h = s // 2, s % 2
-
         @pl.when(s == 0)
         def _():
             hand_c[0][0].wait_recv()
+            hand_a[0].wait_recv()
 
         @pl.when(s == 1)
         def _():
@@ -472,6 +482,7 @@
 
         @pl.when(s == 2)
         def _():
+            fifth(1, 1, p3)
             hand_c[1][0].wait_recv()
             hand_a[1].wait_recv()
 
@@ -479,29 +490,12 @@
         def _():
             hand_c[1][1].wait_recv()
 
-        multiply(w, h, lanes_both, 1)
-
-        @pl.when(s == 0)
-        def _():
-            end_z(steps_a)
-            hand_a[0].wait_recv()
-
-        @pl.when(s == 1)
-        def _():
-            fifth(1, 1, p3)
-
-        multiply(w, h, lanes_a, 2)
-        store(w, h)
+        multiply(s)
         return 0
 
     lax.fori_loop(0, 4, products, 0)
-
-    def finish(m, _):
-        some = pl.ds(pl.multiple_of(m * 1024, 1024), 1024)
-        out_ref[some, :] = outf[some, :].astype(BF16)
-        return 0
-
-    lax.fori_loop(0, 8, finish, 0)
+    for m in range(2):
+        write_back(m).wait()
     for copy in copies.made:
         copy.wait_send()
 
@@ -526,13 +520,12 @@
 def per_device(conduction, valence, resident, interaction):
     weights, chunk_phase, planes, group_phase = (jnp.asarray(t) for t in tables())
     anywhere = pl.BlockSpec(memory_space=pl.ANY)
-    vmem = pl.BlockSpec(memory_space=pltpu.VMEM)
     out = pl.pallas_call(
         kernel,
         name="exchange_row",
         out_shape=jax.ShapeDtypeStruct((8192, 128), BF16),
         in_specs=[anywhere] * 8,
-        out_specs=vmem,
+        out_specs=anywhere,
         scratch_shapes=[
             pltpu.VMEM((2, 12, 2, 288), BF16),
             pltpu.VMEM((KXY, 128), F32),
@@ -552,9 +545,9 @@
             pltpu.VMEM((8, 128, 128), BF16),
             pltpu.VMEM((NZ, NK, 2, NX, NY, 16, 512), BF16),
             pltpu.VMEM((8, 1024, 512), BF16),
-            pltpu.VMEM((2, 2, 1024, 256), F32),
             pltpu.VMEM((8192, 128), F32),
-            pltpu.SemaphoreType.DMA((15,)),
+            pltpu.VMEM((8192, 128), BF16),
+            pltpu.SemaphoreType.DMA((17,)),
             pltpu.SemaphoreType.DMA((N_GROUPS,)),
             pltpu.SemaphoreType.DMA((N_GROUPS,)),
         ],

time: 87.7 us -> 82.9 us (0.945)
  Pallas kernels: 87.6 us -> 82.8 us
    pallas_call x1, Pallas kernels: 85.2 us -> 80.3 us  [per_device(): pl.pallas_call(kernel, name='exchange_row', out_shape=jax.ShapeDtypeStruc...]
where the time goes in v3:
time: 82.9 us; the launch traced here: 82.8 us
  Pallas kernels  82.8 us (100%)
    pallas_call x1, Pallas kernels, per_device(): pl.pallas_call(kernel, name='exchange_row', out_shape=jax.ShapeDtypeStruc...  80.3 us
    pallas_call x1, Pallas kernels, per_device(): pl.pallas_call(write_out, name='write_out', out_shape=jax.ShapeDtypeStruc...  2.42 us

profile of v3, /device:TPU:1, one launch (start us, length us, event | category | flops | bytes accessed | tf_op | source)
XLA Modules:
  0.0 82.8 jit_solution(8154174681625654500)
XLA Ops:
  0.0 80.3 %exchange_row.1.in_ref = bf16[8192,128]{1,0:T(8,128)(2,1)} custom-call(bf16[2,12,16,9216]{3,2,1,0:T(8,128)(2,1)} %bitcast.8, bf16[2,12,2,288]{3,2,1,0:T(2,128)(2,1)} %bitcast.9, bf16[32,2,16,2048]{3,2,1,0:T(8,128)(2,1)} %res_hbm.1, f32[16,128]{1,0:T(8,128)} %bitcast.10, bf16[2304,256]{1,0:T(8,128)(2,1)} %constant.8.clone.w_hbm, ...), custom_call_target="tpu_custom_call" | custom-call | tf_op jit(solution)/shard_map/exchange_row/pallas_call | solution.py:523
  80.3 2.4 %write_out.1 = bf16[8192,128]{1,0:T(8,128)(2,1)} custom-call(bf16[8192,128]{1,0:T(8,128)(2,1)} %exchange_row.1.in_ref), custom_call_target="tpu_custom_call" | custom-call | tf_op jit(solution)/shard_map/write_out/pallas_call | solution.py:567

commit v4 on v3

--- a/solution.py
+++ b/solution.py
@@ -127,6 +127,14 @@
 
     copies = Copies(send_sem, recv_sem, at(dk=1))
 
+    plane_peers = [(i, j) for i in (2, 1, 3, 0) for j in (2, 1, 3, 0) if i or j]
+    peers = [at(dz=d) for d in (4, 3, 5, 2, 6, 1, 7)]
+    peers += [at(dx=i, dy=j) for i, j in plane_peers]
+    peers += [{"val": ((zl + d) % 4) * 2 + (k + 1) % 2, "cond": c} for d in range(4)]
+    barrier = pltpu.get_barrier_semaphore()
+    for peer in peers:
+        pl.semaphore_signal(barrier, 1, device_id=peer, device_id_type=pl.DeviceIdType.MESH)
+
     def chunk_at(j):
         i = j % 4
         return j // 4, (x + i + i // 2 - 2 * (i // 3)) % NX
@@ -154,14 +162,6 @@
     load_plane.start()
     load_res = pltpu.make_async_copy(res_hbm, res_v, local_sem.at[10])
     load_res.start()
-
-    plane_peers = [(i, j) for i in (2, 1, 3, 0) for j in (2, 1, 3, 0) if i or j]
-    peers = [at(dx=i, dy=j) for i, j in plane_peers]
-    peers += [at(dz=d) for d in range(1, 8)]
-    peers += [{"val": ((zl + d) % 4) * 2 + (k + 1) % 2, "cond": c} for d in range(4)]
-    barrier = pltpu.get_barrier_semaphore()
-    for peer in peers:
-        pl.semaphore_signal(barrier, 1, device_id=peer, device_id_type=pl.DeviceIdType.MESH)
 
     load_val.wait()
     block = val_ref[...].astype(F32).reshape(48, 288)
@@ -413,39 +413,30 @@
     factor = 2.0 / math.sqrt(NG)
 
     def multiply(s):
-        w, h = s // 2, s % 2
+        w, h = s % 2, s // 2
         owners = [(i, q) for i in range(4) for q in range(NK)]
 
-        def rows_step(m, _):
-            at_rows = pl.ds(pl.multiple_of(m * 512, 512), 512)
-            rows = jnp.concatenate([left[i * NK + q, at_rows, :] for i, q in owners], axis=1)
-            new = [gath[h * 4 + i, q, w].reshape(256, 512) for i, q in owners]
-            product = factor * lax.dot_general(
-                rows,
-                jnp.concatenate(new, axis=1),
-                (((1,), (1,)), ((), ())),
-                preferred_element_type=F32,
-            )
-            for t in range(2):
-                start = m * 4096 + (h * 2 + t) * 2 + w
-                outf[pl.ds(start, 512, stride=8), :] = product[:, t * 128 : t * 128 + 128]
-
-            @pl.when(s == 3)
-            def _():
-                def finish(i, _):
-                    some = pl.ds(pl.multiple_of(m * 4096 + i * 1024, 1024), 1024)
-                    out_v[some, :] = outf[some, :].astype(BF16)
-                    return 0
-
-                lax.fori_loop(0, 4, finish, 0)
-                write_back(m).start()
-
-            return 0
-
-        lax.fori_loop(0, 2, rows_step, 0)
+        rows = jnp.concatenate([left[i * NK + q] for i, q in owners], axis=1)
+        new = [gath[h * 4 + i, q, w].reshape(256, 512) for i, q in owners]
+        product = factor * lax.dot_general(
+            rows,
+            jnp.concatenate(new, axis=1),
+            (((1,), (1,)), ((), ())),
+            preferred_element_type=F32,
+        )
+        for t in range(2):
+            start = (h * 2 + t) * 2 + w
+            outf[pl.ds(start, 1024, stride=8), :] = product[:, t * 128 : t * 128 + 128]
+
+    def finish(m, _):
+        for i in range(2):
+            some = pl.ds(pl.multiple_of(m * 2048 + i * 1024, 1024), 1024)
+            out_v[some, :] = outf[some, :].astype(BF16)
+        write_back(m).start()
+        return 0
 
     def write_back(m):
-        some = pl.ds(pl.multiple_of(m * 4096, 4096), 4096)
+        some = pl.ds(pl.multiple_of(m * 2048, 2048), 2048)
         return pltpu.make_async_copy(out_v.at[some], out_hbm.at[some], local_sem.at[15 + m])
 
     sends_c, sends_a = first()
@@ -455,18 +446,17 @@
     sends_c = second()
     steps_a = along_z(2, steps_a)
     wait_all(sends_c)
-    p0, p1, p2 = third(0, 0), third(0, 1), third(1, 0)
+    p0, p1, p2 = third(0, 0), third(1, 0), third(0, 1)
     hand_second()
     steps_a = along_z(3, steps_a)
     p0 = fourth(0, 0, p0)
     p3 = third(1, 1)
-    p1 = fourth(0, 1, p1)
+    p1 = fourth(1, 0, p1)
     steps_a = along_z(4, steps_a)
-    p2 = fourth(1, 0, p2)
+    p2 = fourth(0, 1, p2)
     fifth(0, 0, p0)
     p3 = fourth(1, 1, p3)
-    fifth(0, 1, p1)
-
+    fifth(1, 0, p1)
     end_z(steps_a)
 
     def products(s, _):
@@ -477,14 +467,14 @@
 
         @pl.when(s == 1)
         def _():
-            fifth(1, 0, p2)
-            hand_c[0][1].wait_recv()
+            fifth(0, 1, p2)
+            hand_c[1][0].wait_recv()
+            hand_a[1].wait_recv()
 
         @pl.when(s == 2)
         def _():
             fifth(1, 1, p3)
-            hand_c[1][0].wait_recv()
-            hand_a[1].wait_recv()
+            hand_c[0][1].wait_recv()
 
         @pl.when(s == 3)
         def _():
@@ -494,7 +484,8 @@
         return 0
 
     lax.fori_loop(0, 4, products, 0)
-    for m in range(2):
+    lax.fori_loop(0, 4, finish, 0)
+    for m in range(4):
         write_back(m).wait()
     for copy in copies.made:
         copy.wait_send()
@@ -547,7 +538,7 @@
             pltpu.VMEM((8, 1024, 512), BF16),
             pltpu.VMEM((8192, 128), F32),
             pltpu.VMEM((8192, 128), BF16),
-            pltpu.SemaphoreType.DMA((17,)),
+            pltpu.SemaphoreType.DMA((19,)),
             pltpu.SemaphoreType.DMA((N_GROUPS,)),
             pltpu.SemaphoreType.DMA((N_GROUPS,)),
         ],

time: 82.9 us -> 81.9 us (0.988)
  Pallas kernels: 82.8 us -> 81.8 us
    pallas_call x1, Pallas kernels: 80.3 us -> 79.4 us  [per_device(): pl.pallas_call(kernel, name='exchange_row', out_shape=jax.ShapeDtypeStruc...]
where the time goes in v4:
time: 81.9 us; the launch traced here: 81.8 us
  Pallas kernels  81.8 us (100%)
    pallas_call x1, Pallas kernels, per_device(): pl.pallas_call(kernel, name='exchange_row', out_shape=jax.ShapeDtypeStruc...  79.4 us
    pallas_call x1, Pallas kernels, per_device(): pl.pallas_call(write_out, name='write_out', out_shape=jax.ShapeDtypeStruc...  2.42 us

profile of v4, /device:TPU:1, one launch (start us, length us, event | category | flops | bytes accessed | tf_op | source)
XLA Modules:
  0.0 81.8 jit_solution(13061451266322255418)
XLA Ops:
  0.0 79.4 %exchange_row.1.in_ref = bf16[8192,128]{1,0:T(8,128)(2,1)} custom-call(bf16[2,12,16,9216]{3,2,1,0:T(8,128)(2,1)} %bitcast.8, bf16[2,12,2,288]{3,2,1,0:T(2,128)(2,1)} %bitcast.9, bf16[32,2,16,2048]{3,2,1,0:T(8,128)(2,1)} %res_hbm.1, f32[16,128]{1,0:T(8,128)} %bitcast.10, bf16[2304,256]{1,0:T(8,128)(2,1)} %constant.8.clone.w_hbm, ...), custom_call_target="tpu_custom_call" | custom-call | tf_op jit(solution)/shard_map/exchange_row/pallas_call | solution.py:514
  79.4 2.4 %write_out.1 = bf16[8192,128]{1,0:T(8,128)(2,1)} custom-call(bf16[8192,128]{1,0:T(8,128)(2,1)} %exchange_row.1.in_ref), custom_call_target="tpu_custom_call" | custom-call | tf_op jit(solution)/shard_map/write_out/pallas_call | solution.py:558
